TPU v7x, 32 devices: a whole 2x2x4 slice. The times are simulated.
32 devices in a mesh: groups: 2 (over x), dp: 16 (over z, y, core).
Axes of the slice: x: 2, y: 2, z: 4, core: 2. Of those that a mesh axis runs over, the one named last changes fastest.
Arguments:
- acts: bfloat16 [16384, 5120], P(('groups', 'dp')), parts along dimension 0, may hold values from -72 to 72, as said below
- out_grads: bfloat16 [16384, 2560], P(('groups', 'dp')), parts along dimension 0, may hold values from -24 to 24
- a_old: float32 [10240], P(('groups', 'dp')), parts along dimension 0, may hold values from 0.5 to 2
- eigen_old: float32 [5120], P('groups'), parts along dimension 0, may hold values from 0.005 to 2
- gradient: float32 [10240, 2560], P(('groups', 'dp')), parts along dimension 0, may hold values from -1.75 to 1.75
- basis: bfloat16 [5120, 2560], P(('groups', 'dp')), parts along dimension 0, may hold values from -0.125 to 0.125
Outputs:
- a_new: float32 [10240], P(('groups', 'dp')), parts along dimension 0
- eigen_new: float32 [5120], P('groups'), parts along dimension 0
- update: float32 [10240, 2560], P(('groups', 'dp')), parts along dimension 0
There are 2 independent parts, one for each index of `groups`. A program takes and returns all parts, laid end to end along the dimension named above; each array names one. Nothing has to cross between parts.
Inputs may be any that keep to these rules, and one draw needn't show every extreme that they name: `acts`: each entry is a random feature value times a scale of its token and a scale of its feature.
All inputs are finite; a program needn't handle non-finite values.
Results may differ from a plain program's by a relative error of at most 0.0003.
Values may be sent and summed in bfloat16 or wider, within the bound.
A program may use at most 128 MiB of HBM per device.

v0:
```python
import jax
import jax.numpy as jnp
from jax import lax
from jax.sharding import PartitionSpec as P

RETAIN = 0.9
DAMPING = 0.001


def shards(acts, out_grads, a_old, eigen_old, gradient, basis):
    tokens = acts.shape[0] * lax.axis_size("dp")
    own_rows = a_old.shape[0]
    act_float = acts.astype(jnp.float32)
    act_part = jnp.sum(act_float * act_float, axis=0)
    shard_rows = lax.all_gather(basis, "dp", axis=0, tiled=True)
    token_part = jnp.dot(out_grads, shard_rows, preferred_element_type=jnp.float32)
    row_part = jnp.dot(gradient, shard_rows.astype(jnp.float32), precision=lax.Precision.HIGHEST)
    eigen_part = jnp.sum(token_part * token_part, axis=0)
    act_whole, eigen_total = lax.psum((act_part, eigen_part), "dp")
    act_total = lax.dynamic_slice_in_dim(act_whole, lax.axis_index("dp") * own_rows, own_rows, 0)
    a_new = RETAIN * a_old + (1.0 - RETAIN) * (act_total / tokens)
    eigen_new = RETAIN * eigen_old + (1.0 - RETAIN) * (eigen_total / tokens)
    scaled = row_part / (a_new[:, None] * eigen_new[None, :] + DAMPING)
    update = jnp.einsum(
        "ik,jk->ij",
        scaled,
        lax.all_gather(basis, "dp", axis=0, tiled=True).astype(jnp.float32),
        precision=lax.Precision.HIGHEST,
    )
    return (a_new, eigen_new, update)


def solution(mesh):
    return jax.shard_map(
        shards,
        mesh=mesh,
        in_specs=(
            P(("groups", "dp"), None),
            P(("groups", "dp"), None),
            P(("groups", "dp")),
            P("groups"),
            P(("groups", "dp"), None),
            P(("groups", "dp"), None),
        ),
        out_specs=(P(("groups", "dp")), P("groups"), P(("groups", "dp"), None)),
        check_vma=False,
    )
```

profile of v0, /device:TPU:0, one launch (start us, length us, event | category | flops | bytes accessed | tf_op | source)
XLA Modules:
  0.0 224.9 jit_solution(14895530580963725721)
XLA Ops:
  7.2 0.0 copy-start
  7.2 0.0 all-gather.2.cloned.1.call-start
  7.2 0.7 all-gather.2.cloned.1.call-update
  7.9 3.9 %multiply_reduce_fusion = f32[5120]{0:T(1024)S(1)} fusion(bf16[512,5120]{1,0:T(8,128)(2,1)} %param.6), kind=kLoop, calls=%fused_computation | loop fusion | flops 7859200 | bytes 5263360 | tf_op jit(solution)/shard_map/reduce_sum | solution.py:14
  11.8 0.0 copy-start.1
  11.8 0.0 copy-start.3
  11.8 105.2 %all-gather.2.cloned.1.call-done = bf16[2560,2560]{1,0:T(8,128)(2,1)} async-done(((bf16[160,2560]{1,0:T(8,128)(2,1)}), bf16[2560,2560]{1,0:T(8,128)(2,1)}) %all-gather.2.cloned.1.call-update) | async-done | bytes 13107216 | tf_op jit(solution)/shard_map/all_gather | solution.py:15
  117.1 10.8 %fusion = f32[2560]{0:T(1024)S(1)} fusion(bf16[512,2560]{1,0:T(8,128)(2,1)} %param.7, bf16[2560,2560]{1,0:T(8,128)(2,1)} %all-gather.2.cloned.1.call-done), kind=kOutput, calls=%fused_computation.3 | convolution fusion | flops 6713505280 | bytes 15738880 | tf_op jit(solution)/shard_map/dot_general | solution.py:16
  127.8 58.8 %all-reduce = (f32[5120]{0:T(1024)S(1)}, f32[2560]{0:T(1024)S(1)}) all-reduce(f32[5120]{0:T(1024)S(1)} %multiply_reduce_fusion, f32[2560]{0:T(1024)S(1)} %fusion), channel_id=1, replica_groups=mesh['groups'=2,'dp'=16] {'dp'}, use_global_device_ids=true, to_apply=%region_1.0 | all-reduce | flops 7680 | bytes 61440 | tf_op jit(solution)/shard_map/psum | solution.py:19
  186.6 0.0 copy-done.1
  186.6 0.0 copy-start.2
  186.6 0.0 copy-done.3
  186.6 0.1 multiply_add_fusion.1
  186.7 0.0 copy-done
  186.7 0.0 copy-start.4
  186.7 0.0 copy-start.5
  186.7 16.7 %convolution_divide_fusion = f32[320,2560]{1,0:T(8,128)S(1)} fusion(f32[320,2560]{1,0:T(8,128)S(1)} %copy-done, bf16[2560,2560]{1,0:T(8,128)(2,1)} %all-gather.2.cloned.1.call-done, f32[2560]{0:T(1024)S(1)} %multiply_add_fusion, f32[320]{0:T(512)S(1)} %multiply_add_fusion.1), kind=kOutput, calls=%fused_computation.2 | convolution fusion | flops 25168281600 | bytes 19672320 | tf_op jit(solution)/shard_map/dot_general | solution.py:17
  203.4 0.0 copy-done.2
  203.4 0.0 copy-done.4
  203.4 0.0 copy-done.5
  203.4 14.6 %fusion.1 = f32[320,2560]{1,0:T(8,128)} fusion(f32[320,2560]{1,0:T(8,128)S(1)} %convolution_divide_fusion, bf16[2560,2560]{1,0:T(8,128)(2,1)S(1)} %copy-done.5), kind=kOutput, calls=%fused_computation.6 | convolution fusion | flops 25165824000 | bytes 19660800 | tf_op jit(solution)/shard_map/ik,jk->ij/dot_general | solution.py:24
  (1 shorter events, 0.0 us)
Async XLA Ops:
  7.2 179.5 %copy-start = (f32[320,2560]{1,0:T(8,128)S(1)}, f32[320,2560]{1,0:T(8,128)}, u32[]{:S(2)}) copy-start(f32[320,2560]{1,0:T(8,128)} %param.10) | copy-start | bytes 9830404
  7.2 109.9 %all-gather.2.cloned.1.call-start = ((), (), s32[]{:S(2)}) async-start(), calls=%async_computation | async-start | bytes 13926400 | tf_op jit(solution)/shard_map/all_gather | solution.py:15
  11.8 174.8 %copy-start.1 = (f32[2560]{0:T(1024)S(1)}, f32[2560]{0:T(1024)}, u32[]{:S(2)}) copy-start(f32[2560]{0:T(1024)} %param.9) | copy-start | bytes 30724
  11.8 174.8 %copy-start.3 = (f32[320]{0:T(512)S(1)}, f32[320]{0:T(512)}, u32[]{:S(2)}) copy-start(f32[320]{0:T(512)} %param.8) | copy-start | bytes 3844
  186.6 16.8 %copy-start.2 = (f32[2560]{0:T(1024)}, f32[2560]{0:T(1024)S(1)}, u32[]{:S(2)}) copy-start(f32[2560]{0:T(1024)S(1)} %multiply_add_fusion) | copy-start | bytes 30724
  186.7 16.7 %copy-start.4 = (f32[320]{0:T(512)}, f32[320]{0:T(512)S(1)}, u32[]{:S(2)}) copy-start(f32[320]{0:T(512)S(1)} %multiply_add_fusion.1) | copy-start | bytes 3844
  186.7 16.7 %copy-start.5 = (bf16[2560,2560]{1,0:T(8,128)(2,1)S(1)}, bf16[2560,2560]{1,0:T(8,128)(2,1)}, u32[]{:S(2)}) copy-start(bf16[2560,2560]{1,0:T(8,128)(2,1)} %all-gather.2.cloned.1.call-done) | copy-start | bytes 39321604
Sparse Core Ops, SparseCore 0:
  10.3 106.7 all-gather.1
where the time goes:
time: 225 us
  waiting for transfers between devices  106 us (47%)
  blocking collectives  58.8 us (26%)
  matrix products  42 us (19%)
  between operations  14.1 us (6%)
  other arithmetic  3.96 us (2%)
    all_gather x1, waiting for transfers between devices, shards(): shard_rows = lax.all_gather(basis, 'dp', axis=0, tiled=True)  105 us
    psum x1, blocking collectives, shards(): act_whole, eigen_total = lax.psum((act_part, eigen_part), 'dp')  58.8 us
    dot_general x1, matrix products, shards(): jnp.dot(gradient, shard_rows.astype(jnp.float32), precision=lax.Precision...  16.7 us
    dot_general x1, matrix products, shards(): jnp.einsum('ik,jk->ij', scaled, lax.all_gather(basis, 'dp', axis=0, tiled...  14.6 us
    dot_general x1, matrix products, shards(): jnp.dot(out_grads, shard_rows, preferred_element_type=jnp.float32)  10.8 us
  transfers between devices with their start and end apart: 1, of which 1 were waited for; matrix products, arithmetic and copies ran while one was open for 2% of the time, Pallas kernels for 0%

commit v1 on v0

--- a/solution.py
+++ b/solution.py
@@ -1,13 +1,330 @@
+import functools
+
 import jax
 import jax.numpy as jnp
 from jax import lax
+from jax.experimental import pallas as pl
+from jax.experimental.pallas import tpu as pltpu
 from jax.sharding import PartitionSpec as P
 
 RETAIN = 0.9
 DAMPING = 0.001
-
-
-def shards(acts, out_grads, a_old, eigen_old, gradient, basis):
+MESH = pl.DeviceIdType.MESH
+CHUNKS = 5
+AHEAD = 2
+
+
+def split(x):
+    high = x.astype(jnp.bfloat16)
+    low = (x - high.astype(jnp.float32)).astype(jnp.bfloat16)
+    return high, low
+
+
+def kernel(
+    n, tokens, acts_hbm, grads_hbm, rows_hbm, a_old, eigen_old, basis,
+    a_new, eigen_new, update,
+    whole, acts, lhs, rows, coeffs, damped, column, act_sums, eigen_sums,
+    load_sem, send_sem, recv_sem, act_send, act_recv, eigen_send, eigen_recv,
+):
+    me = lax.axis_index("dp")
+    group = lax.axis_index("groups")
+    core = me % 2
+    side = (me // 2) % 2
+    layer = me // 4
+    layers = n // 4
+    height, features = basis.shape
+    width = features // CHUNKS
+    local_tokens = grads_hbm.shape[0]
+    local_rows = rows_hbm.shape[0]
+
+    def index(at_layer, at_side, at_core):
+        return (at_layer * 2 + at_side) * 2 + at_core
+
+    sibling = index(layer, side, 1 - core)
+    across = index(layer, 1 - side, core)
+
+    load_acts = pltpu.make_async_copy(acts_hbm, acts, load_sem.at[0])
+    load_grads = pltpu.make_async_copy(grads_hbm, lhs.at[pl.ds(0, local_tokens), :], load_sem.at[1])
+    load_rows = pltpu.make_async_copy(rows_hbm, rows, load_sem.at[2])
+
+    barrier = pltpu.get_barrier_semaphore()
+
+    def greet(d, _):
+        pl.semaphore_signal(barrier, inc=1, device_id=(group, (me + d) % n), device_id_type=MESH)
+        return _
+
+    lax.fori_loop(1, n, greet, 0)
+    load_acts.start()
+    load_grads.start()
+    load_rows.start()
+    pl.semaphore_wait(barrier, n - 1)
+
+    def slot(c, owner):
+        return whole.at[c, pl.ds(pl.multiple_of(owner * height, 16), height), :]
+
+    def move(c, owner, target, which, own=False):
+        source = basis.at[:, pl.ds(pl.multiple_of(c * width, 128), width)] if own else slot(c, owner)
+        return pltpu.make_async_remote_copy(
+            src_ref=source,
+            dst_ref=slot(c, owner),
+            send_sem=send_sem.at[c, which],
+            recv_sem=recv_sem.at[c, owner],
+            device_id=(group, target),
+            device_id_type=MESH,
+        )
+
+    def own_moves(c):
+        moves = [move(c, me, index((layer + d) % layers, side, core), d - 1, True) for d in range(1, layers)]
+        moves.append(move(c, me, across, layers - 1, True))
+        moves.append(move(c, me, sibling, layers, True))
+        return moves
+
+    def layer_moves(c):
+        out = []
+        for d in range(1, layers):
+            owner = index((layer + layers - d) % layers, side, core)
+            base = layers + 1 + 2 * (d - 1)
+            out.append((move(c, owner, across, base), move(c, owner, sibling, base + 1)))
+        return out
+
+    def across_moves(c):
+        base = layers + 1 + 2 * (layers - 1)
+        return [
+            move(c, index((layer + layers - d) % layers, 1 - side, core), sibling, base + d)
+            for d in range(layers)
+        ]
+
+    def send_own(c):
+        for copy in own_moves(c):
+            copy.start()
+        whole[c, pl.ds(pl.multiple_of(me * height, 16), height), :] = basis[
+            :, pl.ds(pl.multiple_of(c * width, 128), width)
+        ]
+
+    for c in range(AHEAD):
+        send_own(c)
+
+    load_acts.wait()
+    act_width = 512
+
+    def add_acts(b, _):
+        columns = pl.ds(pl.multiple_of(b * act_width, 128), act_width)
+        block = acts[:, columns].astype(jnp.float32)
+        act_sums[me, :, columns] = jnp.sum(block * block, axis=0, keepdims=True)
+        return _
+
+    lax.fori_loop(0, acts.shape[1] // act_width, add_acts, 0)
+
+    def act_copy(d, owner):
+        return pltpu.make_async_remote_copy(
+            src_ref=act_sums.at[owner],
+            dst_ref=act_sums.at[owner],
+            send_sem=act_send.at[d],
+            recv_sem=act_recv.at[owner],
+            device_id=(group, (me + d) % n),
+            device_id_type=MESH,
+        )
+
+    def eigen_copy(c, d, owner):
+        return pltpu.make_async_remote_copy(
+            src_ref=eigen_sums.at[c, owner],
+            dst_ref=eigen_sums.at[c, owner],
+            send_sem=eigen_send.at[c, d],
+            recv_sem=eigen_recv.at[c, owner],
+            device_id=(group, (me + d) % n),
+            device_id_type=MESH,
+        )
+
+    def send_acts(d, _):
+        act_copy(d, me).start()
+        return _
+
+    lax.fori_loop(1, n, send_acts, 0)
+
+    load_rows.wait()
+    high, low = split(rows[...])
+    lhs[pl.ds(local_tokens, local_rows), :] = high
+    lhs[pl.ds(local_tokens + local_rows, local_rows), :] = low
+    load_grads.wait()
+    update[...] = jnp.zeros_like(update)
+
+    def rotate(c):
+        tile = 256
+
+        def part(t, _):
+            columns = pl.ds(pl.multiple_of(t * tile, 128), tile)
+            out = jnp.dot(lhs[...], whole[c, :, columns], preferred_element_type=jnp.float32)
+            turned = out[:local_tokens]
+            eigen_sums[c, me, :, columns] = jnp.sum(turned * turned, axis=0, keepdims=True)
+            coeffs[c, :, columns] = out[local_tokens : local_tokens + local_rows] + out[local_tokens + local_rows :]
+            return _
+
+        lax.fori_loop(0, width // tile, part, 0)
+
+        def send(d, _):
+            eigen_copy(c, d, me).start()
+            return _
+
+        lax.fori_loop(1, n, send, 0)
+
+    def finish_acts():
+        def arrive(d, _):
+            act_copy(d, (me + n - d) % n).wait_recv()
+            return _
+
+        lax.fori_loop(1, n, arrive, 0)
+        total = act_sums[0]
+        for owner in range(1, n):
+            total = total + act_sums[owner]
+        wide = total.shape[1]
+        block = 512
+        picked = jnp.zeros((local_rows, 1), jnp.float32)
+        for b in range(wide // block):
+            at = lax.broadcasted_iota(jnp.int32, (local_rows, block), 1) + b * block
+            row = lax.broadcasted_iota(jnp.int32, (local_rows, block), 0) + me * local_rows
+            mine = jnp.where(at == row, jnp.broadcast_to(total[:, b * block : (b + 1) * block], at.shape), 0.0)
+            picked = picked + jnp.sum(mine, axis=1, keepdims=True)
+        square = (local_rows, local_rows)
+        same = lax.broadcasted_iota(jnp.int32, square, 0) == lax.broadcasted_iota(jnp.int32, square, 1)
+        old = jnp.sum(jnp.where(same, jnp.broadcast_to(a_old[...], square), 0.0), axis=1, keepdims=True)
+        new = RETAIN * old + (1.0 - RETAIN) * (picked / tokens)
+        column[...] = jnp.broadcast_to(new, column.shape)
+        a_new[...] = jnp.sum(jnp.where(same, jnp.broadcast_to(new, square), 0.0), axis=0, keepdims=True)
+
+    def back(c):
+        def arrive(d, _):
+            eigen_copy(c, d, (me + n - d) % n).wait_recv()
+            return _
+
+        lax.fori_loop(1, n, arrive, 0)
+        total = eigen_sums[c, 0]
+        for owner in range(1, n):
+            total = total + eigen_sums[c, owner]
+        columns = pl.ds(pl.multiple_of(c * width, 128), width)
+        values = RETAIN * eigen_old[:, columns] + (1.0 - RETAIN) * (total / tokens)
+        eigen_new[:, columns] = values
+        scaled = coeffs[c] / (column[:, 0:1] * values + DAMPING)
+        top, bottom = split(scaled)
+        damped[pl.ds(0, local_rows), :] = top
+        damped[pl.ds(local_rows, local_rows), :] = bottom
+        tile = 256
+
+        def part(t, _):
+            here = pl.ds(pl.multiple_of(t * tile, 128), tile)
+            out = lax.dot_general(
+                damped[...], whole[c, here, :], (((1,), (1,)), ((), ())), preferred_element_type=jnp.float32
+            )
+            update[:, here] += out[:local_rows] + out[local_rows:]
+            return _
+
+        lax.fori_loop(0, features // tile, part, 0)
+
+    def step(i, carry):
+        @pl.when(i < CHUNKS)
+        def _():
+            for over, beside in layer_moves(i):
+                over.wait_recv()
+                over.start()
+                beside.start()
+
+        @pl.when(i + AHEAD < CHUNKS)
+        def _():
+            send_own(i + AHEAD)
+
+        @pl.when(jnp.logical_and(i >= 1, i <= CHUNKS))
+        def _():
+            c = i - 1
+            for copy in across_moves(c):
+                copy.wait_recv()
+                copy.start()
+            for at_side in range(2):
+                for d in range(layers):
+                    owner = index(d, at_side, 1 - core)
+                    move(c, owner, sibling, 0).wait_recv()
+            rotate(c)
+
+        @pl.when(i == 1)
+        def _():
+            finish_acts()
+
+        @pl.when(i >= 2)
+        def _():
+            back(i - 2)
+
+        return carry
+
+    lax.fori_loop(0, CHUNKS + 2, step, 0)
+
+    def drain(c, _):
+        for copy in own_moves(c):
+            copy.wait_send()
+        for over, beside in layer_moves(c):
+            over.wait_send()
+            beside.wait_send()
+        for copy in across_moves(c):
+            copy.wait_send()
+
+        def sent(d, _):
+            eigen_copy(c, d, me).wait_send()
+            return _
+
+        return lax.fori_loop(1, n, sent, _)
+
+    lax.fori_loop(0, CHUNKS, drain, 0)
+
+    def act_sent(d, _):
+        act_copy(d, me).wait_send()
+        return _
+
+    lax.fori_loop(1, n, act_sent, 0)
+
+
+def fused(acts, out_grads, a_old, eigen_old, gradient, basis):
+    n = lax.axis_size("dp")
+    tokens = acts.shape[0] * n
+    height, features = basis.shape
+    width = features // CHUNKS
+    local_rows = gradient.shape[0]
+    depth = out_grads.shape[0] + 2 * local_rows
+    wide = acts.shape[1]
+    hbm = pl.BlockSpec(memory_space=pl.ANY)
+    vmem = pl.BlockSpec(memory_space=pltpu.VMEM)
+    copies = 4 * (n // 4)
+    a_new, eigen_new, update = pl.pallas_call(
+        functools.partial(kernel, n, tokens),
+        out_shape=(
+            jax.ShapeDtypeStruct((1, local_rows), jnp.float32),
+            jax.ShapeDtypeStruct((1, features), jnp.float32),
+            jax.ShapeDtypeStruct((local_rows, features), jnp.float32),
+        ),
+        in_specs=[hbm, hbm, hbm, vmem, vmem, vmem],
+        out_specs=(vmem, vmem, vmem),
+        scratch_shapes=[
+            pltpu.VMEM((CHUNKS, features, width), jnp.bfloat16),
+            pltpu.VMEM(acts.shape, jnp.bfloat16),
+            pltpu.VMEM((depth, features), jnp.bfloat16),
+            pltpu.VMEM(gradient.shape, jnp.float32),
+            pltpu.VMEM((CHUNKS, local_rows, width), jnp.float32),
+            pltpu.VMEM((2 * local_rows, width), jnp.bfloat16),
+            pltpu.VMEM((local_rows, 128), jnp.float32),
+            pltpu.VMEM((n, 1, wide), jnp.float32),
+            pltpu.VMEM((CHUNKS, n, 1, width), jnp.float32),
+            pltpu.SemaphoreType.DMA((3,)),
+            pltpu.SemaphoreType.DMA((CHUNKS, copies)),
+            pltpu.SemaphoreType.DMA((CHUNKS, n)),
+            pltpu.SemaphoreType.DMA((n,)),
+            pltpu.SemaphoreType.DMA((n,)),
+            pltpu.SemaphoreType.DMA((CHUNKS, n)),
+            pltpu.SemaphoreType.DMA((CHUNKS, n)),
+        ],
+        compiler_params=pltpu.CompilerParams(
+            collective_id=0, has_side_effects=True, vmem_limit_bytes=56 * 1024 * 1024
+        ),
+    )(acts, out_grads, gradient, a_old.reshape(1, -1), eigen_old.reshape(1, -1), basis)
+    return a_new.reshape(-1), eigen_new.reshape(-1), update
+
+
+def plain(acts, out_grads, a_old, eigen_old, gradient, basis):
     tokens = acts.shape[0] * lax.axis_size("dp")
     own_rows = a_old.shape[0]
     act_float = acts.astype(jnp.float32)
@@ -21,18 +338,13 @@
     a_new = RETAIN * a_old + (1.0 - RETAIN) * (act_total / tokens)
     eigen_new = RETAIN * eigen_old + (1.0 - RETAIN) * (eigen_total / tokens)
     scaled = row_part / (a_new[:, None] * eigen_new[None, :] + DAMPING)
-    update = jnp.einsum(
-        "ik,jk->ij",
-        scaled,
-        lax.all_gather(basis, "dp", axis=0, tiled=True).astype(jnp.float32),
-        precision=lax.Precision.HIGHEST,
-    )
+    update = jnp.einsum("ik,jk->ij", scaled, shard_rows.astype(jnp.float32), precision=lax.Precision.HIGHEST)
     return (a_new, eigen_new, update)
 
 
 def solution(mesh):
     return jax.shard_map(
-        shards,
+        fused if mesh.shape["dp"] == 16 else plain,
         mesh=mesh,
         in_specs=(
             P(("groups", "dp"), None),

time: 225 us -> 137 us (0.61)
  Pallas kernels: 0 us -> 126 us
  waiting for transfers between devices: 106 us -> 0 us
  blocking collectives: 58.8 us -> 0 us
  matrix products: 42 us -> 0 us
  between operations: 14.1 us -> 0.64 us
  local copies, waits for them, and re-layouts: 0.04 us -> 6.41 us
    pallas_call x0 -> x1, Pallas kernels: none -> 126 us  [fused(): pl.pallas_call(functools.partial(kernel, n, tokens), out_shape=(jax.Shape...]
    all_gather x1 -> x0, waiting for transfers between devices: 105 us -> none  [shards(): shard_rows = lax.all_gather(basis, 'dp', axis=0, tiled=True)]
    psum x1 -> x0, blocking collectives: 58.8 us -> none  [shards(): act_whole, eigen_total = lax.psum((act_part, eigen_part), 'dp')]
    dot_general x3 -> x0, matrix products: 42 us -> none  [the longest x1 16.7 us: shards(): jnp.dot(gradient, shard_rows.astype(jnp.float32), precision=lax.Precision...]
    reduce_sum x1 -> x0, other arithmetic: 3.87 us -> none  [shards(): act_part = jnp.sum(act_float * act_float, axis=0)]
    unnamed x12 -> x1, local copies, waits for them, and re-layouts: 0.04 us -> 3.85 us
    reshape x0 -> x2, local copies, waits for them, and re-layouts: none -> 2.56 us  [the longest x1 1.31 us: fused(): eigen_old.reshape(1, -1)]
    pallas_call x0 -> x2, other arithmetic: none -> 2.55 us  [fused(): pl.pallas_call(functools.partial(kernel, n, tokens), out_shape=(jax.Shape...]
  transfers between devices with their start and end apart: 1 -> 0, of which waited for: 1 -> 0; matrix products, arithmetic and copies ran while one was open for 2% -> 0% of each run, Pallas kernels for 0% -> 0%
where the time goes in v1:
time: 137 us; the launch traced here: 136 us
  Pallas kernels  126 us (92%)
  local copies, waits for them, and re-layouts  6.41 us (5%)
  other arithmetic  2.55 us (2%)
    pallas_call x1, Pallas kernels, fused(): pl.pallas_call(functools.partial(kernel, n, tokens), out_shape=(jax.Shape...  126 us
    unnamed x1, local copies, waits for them, and re-layouts  3.85 us

profile of v1, /device:TPU:0, one launch (start us, length us, event | category | flops | bytes accessed | tf_op | source)
XLA Modules:
  0.0 135.9 jit_solution(10417123093174379201)
XLA Ops:
  0.6 1.3 reshape.19.eigen_old
  1.9 1.2 reshape.18.a_old
  3.2 126.3 %shard_map.85 = (f32[1,320]{1,0:T(1,128)}, f32[1,2560]{1,0:T(1,128)}, f32[320,2560]{1,0:T(8,128)}) custom-call(bf16[512,5120]{1,0:T(8,128)(2,1)} %acts_hbm.1, bf16[512,2560]{1,0:T(8,128)(2,1)} %grads_hbm.1, f32[320,2560]{1,0:T(8,128)} %rows_hbm.1, f32[1,320]{1,0:T(1,128)} %reshape.18.a_old, f32[1,2560]{1,0:T(1,128)} %reshape.19.eigen_old, ...), custom_call_target="tpu_custom_call" | custom-call | tf_op jit(solution)/shard_map/pallas_call | solution.py:293
  129.5 1.3 reduce.1
  130.9 1.2 reduce
  132.1 3.9 %copy.10 = f32[320,2560]{1,0:T(8,128)} copy(f32[320,2560]{1,0:T(8,128)} %get-tuple-element.14) | data formatting | bytes 6553600

commit v2 on v1

--- a/solution.py
+++ b/solution.py
@@ -74,32 +74,55 @@
         )
 
     def own_moves(c):
-        moves = [move(c, me, index((layer + d) % layers, side, core), d - 1, True) for d in range(1, layers)]
-        moves.append(move(c, me, across, layers - 1, True))
-        moves.append(move(c, me, sibling, layers, True))
-        return moves
+        return [
+            (layer < layers - 1, move(c, me, me + 4, 0, True)),
+            (layer > 0, move(c, me, me - 4, 1, True)),
+            (None, move(c, me, across, 2, True)),
+            (None, move(c, me, sibling, 3, True)),
+        ]
 
     def layer_moves(c):
         out = []
         for d in range(1, layers):
-            owner = index((layer + layers - d) % layers, side, core)
-            base = layers + 1 + 2 * (d - 1)
-            out.append((move(c, owner, across, base), move(c, owner, sibling, base + 1)))
+            for below in (True, False):
+                base = 4 + 3 * (2 * (d - 1) + (0 if below else 1))
+                owner = me - 4 * d if below else me + 4 * d
+                onward = me + 4 if below else me - 4
+                present = layer >= d if below else layer + d < layers
+                further = layer < layers - 1 if below else layer > 0
+                out.append((
+                    present,
+                    jnp.logical_and(present, further),
+                    move(c, owner, onward, base),
+                    move(c, owner, across, base + 1),
+                    move(c, owner, sibling, base + 2),
+                ))
         return out
 
     def across_moves(c):
-        base = layers + 1 + 2 * (layers - 1)
+        base = 4 + 6 * (layers - 1)
         return [
             move(c, index((layer + layers - d) % layers, 1 - side, core), sibling, base + d)
             for d in range(layers)
         ]
 
+    def run(condition, action):
+        if condition is None:
+            action()
+        else:
+            pl.when(condition)(action)
+
     def send_own(c):
-        for copy in own_moves(c):
-            copy.start()
+        for condition, copy in own_moves(c):
+            run(condition, copy.start)
         whole[c, pl.ds(pl.multiple_of(me * height, 16), height), :] = basis[
             :, pl.ds(pl.multiple_of(c * width, 128), width)
         ]
+
+    def pass_on(over, beside):
+        over.wait_recv()
+        over.start()
+        beside.start()
 
     for c in range(AHEAD):
         send_own(c)
@@ -222,10 +245,9 @@
     def step(i, carry):
         @pl.when(i < CHUNKS)
         def _():
-            for over, beside in layer_moves(i):
-                over.wait_recv()
-                over.start()
-                beside.start()
+            for present, further, onward, over, beside in layer_moves(i):
+                run(present, functools.partial(pass_on, over, beside))
+                run(further, onward.start)
 
         @pl.when(i + AHEAD < CHUNKS)
         def _():
@@ -256,11 +278,12 @@
     lax.fori_loop(0, CHUNKS + 2, step, 0)
 
     def drain(c, _):
-        for copy in own_moves(c):
-            copy.wait_send()
-        for over, beside in layer_moves(c):
-            over.wait_send()
-            beside.wait_send()
+        for condition, copy in own_moves(c):
+            run(condition, copy.wait_send)
+        for present, further, onward, over, beside in layer_moves(c):
+            run(present, over.wait_send)
+            run(present, beside.wait_send)
+            run(further, onward.wait_send)
         for copy in across_moves(c):
             copy.wait_send()
 
@@ -289,7 +312,7 @@
     wide = acts.shape[1]
     hbm = pl.BlockSpec(memory_space=pl.ANY)
     vmem = pl.BlockSpec(memory_space=pltpu.VMEM)
-    copies = 4 * (n // 4)
+    copies = 7 * (n // 4)
     a_new, eigen_new, update = pl.pallas_call(
         functools.partial(kernel, n, tokens),
         out_shape=(

time: 137 us -> 121 us (0.88)
  Pallas kernels: 126 us -> 111 us
    pallas_call x1, Pallas kernels: 126 us -> 111 us  [fused(): pl.pallas_call(functools.partial(kernel, n, tokens), out_shape=(jax.Shape...]
where the time goes in v2:
time: 121 us
  Pallas kernels  111 us (92%)
  local copies, waits for them, and re-layouts  6.41 us (5%)
  other arithmetic  2.55 us (2%)
    pallas_call x1, Pallas kernels, fused(): pl.pallas_call(functools.partial(kernel, n, tokens), out_shape=(jax.Shape...  111 us
    unnamed x1, local copies, waits for them, and re-layouts  3.85 us
    pallas_call x2, other arithmetic, fused(): pl.pallas_call(functools.partial(kernel, n, tokens), out_shape=(jax.Shape...  2.55 us

profile of v2, /device:TPU:0, one launch (start us, length us, event | category | flops | bytes accessed | tf_op | source)
XLA Modules:
  0.0 120.8 jit_solution(3566090878958320692)
XLA Ops:
  0.6 1.3 %reshape.19.eigen_old = f32[1,2560]{1,0:T(1,128)} reshape(f32[2560]{0:T(1024)} %param.9) | data formatting | bytes 20480 | tf_op jit(solution)/shard_map/reshape | solution.py:346
  1.9 1.2 %reshape.18.a_old = f32[1,320]{1,0:T(1,128)} reshape(f32[320]{0:T(512)} %param.8) | data formatting | bytes 2560 | tf_op jit(solution)/shard_map/reshape | solution.py:346
  3.2 111.2 %shard_map.85 = (f32[1,320]{1,0:T(1,128)}, f32[1,2560]{1,0:T(1,128)}, f32[320,2560]{1,0:T(8,128)}) custom-call(bf16[512,5120]{1,0:T(8,128)(2,1)} %acts_hbm.1, bf16[512,2560]{1,0:T(8,128)(2,1)} %grads_hbm.1, f32[320,2560]{1,0:T(8,128)} %rows_hbm.1, f32[1,320]{1,0:T(1,128)} %reshape.18.a_old, f32[1,2560]{1,0:T(1,128)} %reshape.19.eigen_old, ...), custom_call_target="tpu_custom_call" | custom-call | tf_op jit(solution)/shard_map/pallas_call | solution.py:316
  114.3 1.3 %reduce.1 = f32[2560]{0:T(1024)} reduce(f32[1,2560]{1,0:T(1,128)} %get-tuple-element.7, f32[]{:T(128)} %constant), dimensions={0}, to_apply=%get-tuple-element.7.reduce_sub_computation | reduce | bytes 20484 | tf_op jit(solution)/shard_map/pallas_call | solution.py:316
  115.7 1.2 %reduce = f32[320]{0:T(512)} reduce(f32[1,320]{1,0:T(1,128)} %get-tuple-element.6, f32[]{:T(128)} %constant), dimensions={0}, to_apply=%get-tuple-element.6.reduce_sub_computation | reduce | bytes 2564 | tf_op jit(solution)/shard_map/pallas_call | solution.py:316
  116.9 3.9 %copy.10 = f32[320,2560]{1,0:T(8,128)} copy(f32[320,2560]{1,0:T(8,128)} %get-tuple-element.14) | data formatting | bytes 6553600

commit v3 on v2

--- a/solution.py
+++ b/solution.py
@@ -12,6 +12,7 @@
 MESH = pl.DeviceIdType.MESH
 CHUNKS = 5
 AHEAD = 2
+BACK = 2
 
 
 def split(x):
@@ -20,10 +21,14 @@
     return high, low
 
 
+def span(rows):
+    return (rows + 64 + 127) // 128 * 128
+
+
 def kernel(
     n, tokens, acts_hbm, grads_hbm, rows_hbm, a_old, eigen_old, basis,
     a_new, eigen_new, update,
-    whole, acts, lhs, rows, coeffs, damped, column, act_sums, eigen_sums,
+    whole, acts, lhs, rows, coeffs, damped, column, act_row, act_sums, eigen_sums,
     load_sem, send_sem, recv_sem, act_send, act_recv, eigen_send, eigen_recv,
 ):
     me = lax.axis_index("dp")
@@ -53,10 +58,10 @@
         pl.semaphore_signal(barrier, inc=1, device_id=(group, (me + d) % n), device_id_type=MESH)
         return _
 
+    load_acts.start()
+    load_rows.start()
+    load_grads.start()
     lax.fori_loop(1, n, greet, 0)
-    load_acts.start()
-    load_grads.start()
-    load_rows.start()
     pl.semaphore_wait(barrier, n - 1)
 
     def slot(c, owner):
@@ -119,8 +124,9 @@
             :, pl.ds(pl.multiple_of(c * width, 128), width)
         ]
 
-    def pass_on(over, beside):
+    def pass_on(over, beside, further, onward):
         over.wait_recv()
+        run(further, onward.start)
         over.start()
         beside.start()
 
@@ -133,14 +139,18 @@
     def add_acts(b, _):
         columns = pl.ds(pl.multiple_of(b * act_width, 128), act_width)
         block = acts[:, columns].astype(jnp.float32)
-        act_sums[me, :, columns] = jnp.sum(block * block, axis=0, keepdims=True)
+        act_row[:, columns] = jnp.sum(block * block, axis=0, keepdims=True)
         return _
 
     lax.fori_loop(0, acts.shape[1] // act_width, add_acts, 0)
+
+    def window(device):
+        start = (device * local_rows) // 128 * 128
+        return pl.ds(pl.multiple_of(start, 128), span(local_rows))
 
     def act_copy(d, owner):
         return pltpu.make_async_remote_copy(
-            src_ref=act_sums.at[owner],
+            src_ref=act_row.at[:, window((me + d) % n)],
             dst_ref=act_sums.at[owner],
             send_sem=act_send.at[d],
             recv_sem=act_recv.at[owner],
@@ -163,15 +173,17 @@
         return _
 
     lax.fori_loop(1, n, send_acts, 0)
-
-    load_rows.wait()
-    high, low = split(rows[...])
-    lhs[pl.ds(local_tokens, local_rows), :] = high
-    lhs[pl.ds(local_tokens + local_rows, local_rows), :] = low
-    load_grads.wait()
-    update[...] = jnp.zeros_like(update)
-
-    def rotate(c):
+    act_sums[me] = act_row[:, window(me)]
+
+    def prepare():
+        load_rows.wait()
+        high, low = split(rows[...])
+        lhs[pl.ds(local_tokens, local_rows), :] = high
+        lhs[pl.ds(local_tokens + local_rows, local_rows), :] = low
+        load_grads.wait()
+        update[...] = jnp.zeros_like(update)
+
+    def rotate(c, first, last):
         tile = 256
 
         def part(t, _):
@@ -182,8 +194,9 @@
             coeffs[c, :, columns] = out[local_tokens : local_tokens + local_rows] + out[local_tokens + local_rows :]
             return _
 
-        lax.fori_loop(0, width // tile, part, 0)
-
+        lax.fori_loop(first, last, part, 0)
+
+    def share(c):
         def send(d, _):
             eigen_copy(c, d, me).start()
             return _
@@ -199,14 +212,10 @@
         total = act_sums[0]
         for owner in range(1, n):
             total = total + act_sums[owner]
-        wide = total.shape[1]
-        block = 512
-        picked = jnp.zeros((local_rows, 1), jnp.float32)
-        for b in range(wide // block):
-            at = lax.broadcasted_iota(jnp.int32, (local_rows, block), 1) + b * block
-            row = lax.broadcasted_iota(jnp.int32, (local_rows, block), 0) + me * local_rows
-            mine = jnp.where(at == row, jnp.broadcast_to(total[:, b * block : (b + 1) * block], at.shape), 0.0)
-            picked = picked + jnp.sum(mine, axis=1, keepdims=True)
+        shape = (local_rows, total.shape[1])
+        at = lax.broadcasted_iota(jnp.int32, shape, 1) + (me * local_rows) // 128 * 128
+        row = lax.broadcasted_iota(jnp.int32, shape, 0) + me * local_rows
+        picked = jnp.sum(jnp.where(at == row, jnp.broadcast_to(total, shape), 0.0), axis=1, keepdims=True)
         square = (local_rows, local_rows)
         same = lax.broadcasted_iota(jnp.int32, square, 0) == lax.broadcasted_iota(jnp.int32, square, 1)
         old = jnp.sum(jnp.where(same, jnp.broadcast_to(a_old[...], square), 0.0), axis=1, keepdims=True)
@@ -242,40 +251,63 @@
 
         lax.fori_loop(0, features // tile, part, 0)
 
+    def forward(c, first, last):
+        for present, further, onward, over, beside in layer_moves(c)[2 * first : 2 * last]:
+            run(present, functools.partial(pass_on, over, beside, further, onward))
+
     def step(i, carry):
-        @pl.when(i < CHUNKS)
-        def _():
-            for present, further, onward, over, beside in layer_moves(i):
-                run(present, functools.partial(pass_on, over, beside))
-                run(further, onward.start)
+        inside = i < CHUNKS
+        turning = jnp.logical_and(i >= 1, i <= CHUNKS)
+
+        @pl.when(inside)
+        def _():
+            forward(i, 0, 1)
 
         @pl.when(i + AHEAD < CHUNKS)
         def _():
             send_own(i + AHEAD)
 
-        @pl.when(jnp.logical_and(i >= 1, i <= CHUNKS))
-        def _():
-            c = i - 1
-            for copy in across_moves(c):
+        @pl.when(i == 0)
+        def _():
+            prepare()
+
+        @pl.when(turning)
+        def _():
+            for copy in across_moves(i - 1):
                 copy.wait_recv()
                 copy.start()
+
+        @pl.when(inside)
+        def _():
+            forward(i, 1, 2)
+
+        @pl.when(turning)
+        def _():
             for at_side in range(2):
                 for d in range(layers):
-                    owner = index(d, at_side, 1 - core)
-                    move(c, owner, sibling, 0).wait_recv()
-            rotate(c)
+                    move(i - 1, index(d, at_side, 1 - core), sibling, 0).wait_recv()
+            rotate(i - 1, 0, 1)
+
+        @pl.when(inside)
+        def _():
+            forward(i, 2, 3)
+
+        @pl.when(turning)
+        def _():
+            rotate(i - 1, 1, width // 256)
+            share(i - 1)
 
         @pl.when(i == 1)
         def _():
             finish_acts()
 
-        @pl.when(i >= 2)
-        def _():
-            back(i - 2)
+        @pl.when(i >= BACK)
+        def _():
+            back(i - BACK)
 
         return carry
 
-    lax.fori_loop(0, CHUNKS + 2, step, 0)
+    lax.fori_loop(0, CHUNKS + BACK, step, 0)
 
     def drain(c, _):
         for condition, copy in own_moves(c):
@@ -330,7 +362,8 @@
             pltpu.VMEM((CHUNKS, local_rows, width), jnp.float32),
             pltpu.VMEM((2 * local_rows, width), jnp.bfloat16),
             pltpu.VMEM((local_rows, 128), jnp.float32),
-            pltpu.VMEM((n, 1, wide), jnp.float32),
+            pltpu.VMEM((1, wide), jnp.float32),
+            pltpu.VMEM((n, 1, span(local_rows)), jnp.float32),
             pltpu.VMEM((CHUNKS, n, 1, width), jnp.float32),
             pltpu.SemaphoreType.DMA((3,)),
             pltpu.SemaphoreType.DMA((CHUNKS, copies)),

time: 121 us -> 114 us (0.942)
  Pallas kernels: 111 us -> 104 us
    pallas_call x1, Pallas kernels: 111 us -> 104 us  [fused(): pl.pallas_call(functools.partial(kernel, n, tokens), out_shape=(jax.Shape...]
where the time goes in v3:
time: 114 us
  Pallas kernels  104 us (91%)
  local copies, waits for them, and re-layouts  6.41 us (6%)
  other arithmetic  2.55 us (2%)
    pallas_call x1, Pallas kernels, fused(): pl.pallas_call(functools.partial(kernel, n, tokens), out_shape=(jax.Shape...  104 us
    unnamed x1, local copies, waits for them, and re-layouts  3.85 us
    pallas_call x2, other arithmetic, fused(): pl.pallas_call(functools.partial(kernel, n, tokens), out_shape=(jax.Shape...  2.55 us

profile of v3, /device:TPU:0, one launch (start us, length us, event | category | flops | bytes accessed | tf_op | source)
XLA Modules:
  0.0 113.9 jit_solution(9783366103969552533)
XLA Ops:
  0.6 1.3 %reshape.19.eigen_old = f32[1,2560]{1,0:T(1,128)} reshape(f32[2560]{0:T(1024)} %param.9) | data formatting | bytes 20480 | tf_op jit(solution)/shard_map/reshape | solution.py:379
  1.9 1.2 %reshape.18.a_old = f32[1,320]{1,0:T(1,128)} reshape(f32[320]{0:T(512)} %param.8) | data formatting | bytes 2560 | tf_op jit(solution)/shard_map/reshape | solution.py:379
  3.2 104.3 %shard_map.85 = (f32[1,320]{1,0:T(1,128)}, f32[1,2560]{1,0:T(1,128)}, f32[320,2560]{1,0:T(8,128)}) custom-call(bf16[512,5120]{1,0:T(8,128)(2,1)} %acts_hbm.1, bf16[512,2560]{1,0:T(8,128)(2,1)} %grads_hbm.1, f32[320,2560]{1,0:T(8,128)} %rows_hbm.1, f32[1,320]{1,0:T(1,128)} %reshape.18.a_old, f32[1,2560]{1,0:T(1,128)} %reshape.19.eigen_old, ...), custom_call_target="tpu_custom_call" | custom-call | tf_op jit(solution)/shard_map/pallas_call | solution.py:348
  107.5 1.3 %reduce.1 = f32[2560]{0:T(1024)} reduce(f32[1,2560]{1,0:T(1,128)} %get-tuple-element.7, f32[]{:T(128)} %constant), dimensions={0}, to_apply=%get-tuple-element.7.reduce_sub_computation | reduce | bytes 20484 | tf_op jit(solution)/shard_map/pallas_call | solution.py:348
  108.9 1.2 %reduce = f32[320]{0:T(512)} reduce(f32[1,320]{1,0:T(1,128)} %get-tuple-element.6, f32[]{:T(128)} %constant), dimensions={0}, to_apply=%get-tuple-element.6.reduce_sub_computation | reduce | bytes 2564 | tf_op jit(solution)/shard_map/pallas_call | solution.py:348
  110.1 3.9 %copy.10 = f32[320,2560]{1,0:T(8,128)} copy(f32[320,2560]{1,0:T(8,128)} %get-tuple-element.14) | data formatting | bytes 6553600
